TPU v7x, 128 devices: a whole 4x4x4 slice. The times are simulated.
128 devices in a mesh: shot: 16 (over z_hi, x, core), slab: 8 (over y, z_lo).
Axes of the slice: x: 4, y: 4, z: 4 (z_hi: 2, z_lo: 2; z = z_hi * 2 + z_lo), core: 2. Of those that a mesh axis runs over, the one named last changes fastest.
Arguments:
- kappa: float32 [128, 256, 256], P('slab', 'shot'), may hold values from 0.05 to 0.25
- buoyancy: float32 [128, 256, 256], P('slab', 'shot'), may hold values from 0.5 to 1
- anchors: int32 [16, 2], replicated, may hold values from 0 to 128
- wave_start: float32 [16, 2, 128, 128, 128], P('shot', None, 'slab'), may hold values from -1.8 to 1.8
- adjoint_start: float32 [16, 2, 128, 128, 128], P('shot', None, 'slab'), may hold values from -1.8 to 1.8
- wavelet: float32 [16, 4], P('shot'), may hold values from -4 to 4
- source_cell: int32 [16, 3], P('shot'), may hold values from 0 to 127
- receiver_cells: int32 [16, 512, 3], P('shot'), may hold values from 0 to 127
- observed: float32 [16, 4, 512], P('shot'), may hold values from -3 to 3
Outputs:
- model_grad: float32 [128, 256, 256], P('slab', 'shot')
- wave_end: float32 [16, 2, 128, 128, 128], P('shot', None, 'slab')
- adjoint_end: float32 [16, 2, 128, 128, 128], P('shot', None, 'slab')
Inputs may be any that keep to these rules, and one draw needn't show every extreme that they name: `anchors`: apertures lie inside the model; several shots' apertures may cover the same cells. `receiver_cells`: several receivers may share a cell.
All inputs are finite; a program needn't handle non-finite values.
Results may differ from a plain program's by a relative error of at most 0.00002.
Values sent between devices are 32-bit elements; how exact they have to be, the bound alone decides.
A program may use at most 128 MiB of HBM per device.

v0:
```python
import jax
import jax.numpy as jnp
from jax import lax
from jax.sharding import PartitionSpec as P

NT = 4


def with_halo(array, sides, width):
    for axis, dim in sides:
        count, length = (lax.axis_size(axis), array.shape[dim])
        up = [(i, (i + 1) % count) for i in range(count - 1)]
        down = [(j, i) for i, j in up]
        last = lax.slice_in_dim(array, length - width, length, axis=dim)
        first = lax.slice_in_dim(array, 0, width, axis=dim)
        before = lax.ppermute(last, axis, up)
        after = lax.ppermute(first, axis, down)
        array = jnp.concatenate([before, array, after], axis=dim)
    return array


def spread_of(field, faces):
    depth_face, row_face, col_face = faces
    pad_depth = with_halo(field, (("slab", 0),), 1)
    flux = depth_face * (pad_depth[1:] - pad_depth[:-1])
    result = flux[1:] - flux[:-1]
    pad_rows = jnp.pad(field, ((0, 0), (1, 1), (0, 0)))
    flux = row_face * (pad_rows[:, 1:] - pad_rows[:, :-1])
    result = result + (flux[:, 1:] - flux[:, :-1])
    pad_cols = jnp.pad(field, ((0, 0), (0, 0), (1, 1)))
    flux = col_face * (pad_cols[:, :, 1:] - pad_cols[:, :, :-1])
    return result + (flux[:, :, 1:] - flux[:, :, :-1])


def add_cells(field, positions, amounts):
    shape = field.shape
    return field.reshape(-1).at[positions].add(amounts).reshape(shape)


def shards(
    kappa,
    buoyancy,
    anchors,
    wave_start,
    adjoint_start,
    wavelet,
    source_cell,
    receiver_cells,
    observed,
):
    depth_cells = kappa.shape[0]
    own_rows = kappa.shape[1]
    model_side = kappa.shape[2]
    aperture = wave_start.shape[3]
    groups = lax.axis_size("shot")
    shot_index = lax.axis_index("shot")
    anchor = anchors[shot_index]
    row_anchor = anchor[0]
    col_anchor = anchor[1]
    stacked = jnp.stack([kappa, buoyancy])
    gathered = lax.all_gather(stacked, "shot", axis=2, tiled=True)
    window = lax.dynamic_slice(
        gathered,
        (row_anchor * 0, row_anchor * 0, row_anchor, col_anchor),
        (2, depth_cells, aperture, aperture),
    )
    kappa_window = window[0]
    buoy_window = window[1]
    padded_buoy = with_halo(buoy_window, (("slab", 0),), 1)
    depth_face = 0.5 * (padded_buoy[1:] + padded_buoy[:-1])
    pad_rows = jnp.pad(buoy_window, ((0, 0), (1, 1), (0, 0)))
    pad_cols = jnp.pad(buoy_window, ((0, 0), (0, 0), (1, 1)))
    row_face = 0.5 * (pad_rows[:, 1:] + pad_rows[:, :-1])
    col_face = 0.5 * (pad_cols[:, :, 1:] + pad_cols[:, :, :-1])
    faces = (depth_face, row_face, col_face)
    depth_start = lax.axis_index("slab") * depth_cells
    receivers = receiver_cells[0]
    local_depth = receivers[:, 0] - depth_start
    receiver_valid = (local_depth >= 0) & (local_depth < depth_cells)
    receiver_flat = (
        jnp.clip(local_depth, 0, depth_cells - 1) * aperture + receivers[:, 1]
    ) * aperture + receivers[:, 2]
    source = source_cell[0]
    source_depth = source[0] - depth_start
    source_valid = (source_depth >= 0) & (source_depth < depth_cells)
    source_flat = (
        jnp.clip(source_depth, 0, depth_cells - 1) * aperture + source[1]
    ) * aperture + source[2]
    before = wave_start[0, 0]
    current = wave_start[0, 1]
    spreads = []
    residuals = []
    for moment in range(NT):
        spread = spread_of(current, faces)
        spreads.append(spread)
        following = 2.0 * current - before + kappa_window * spread
        following = add_cells(
            following, source_flat[None], jnp.where(source_valid, wavelet[0, moment], 0.0)[None]
        )
        sampled = following.reshape(-1)[receiver_flat]
        residuals.append(jnp.where(receiver_valid, sampled - observed[0, moment], 0.0))
        before = current
        current = following
    after = adjoint_start[0, 0]
    later = adjoint_start[0, 1]
    imaging = None
    for moment in reversed(range(NT)):
        adjoint_now = 2.0 * later - after + spread_of(kappa_window * later, faces)
        adjoint_now = add_cells(adjoint_now, receiver_flat, residuals[moment])
        term = adjoint_now * spreads[moment]
        imaging = term if imaging is None else imaging + term
        after = later
        later = adjoint_now
    embedded = lax.dynamic_update_slice(
        jnp.zeros((depth_cells, own_rows * groups, model_side), jnp.float32),
        imaging,
        (row_anchor * 0, row_anchor, col_anchor),
    )
    gradient_rows = lax.psum_scatter(embedded, "shot", scatter_dimension=1, tiled=True)
    return (gradient_rows, jnp.stack([before, current])[None], jnp.stack([after, later])[None])


def solution(mesh):
    in_specs = (
        P("slab", "shot", None),
        P("slab", "shot", None),
        P(),
        P("shot", None, "slab", None, None),
        P("shot", None, "slab", None, None),
        P("shot", None),
        P("shot", None),
        P("shot", None, None),
        P("shot", None, None),
    )
    out_specs = (
        P("slab", "shot", None),
        P("shot", None, "slab", None, None),
        P("shot", None, "slab", None, None),
    )
    return jax.shard_map(shards, mesh=mesh, in_specs=in_specs, out_specs=out_specs, check_vma=False)
```

profile of v0, /device:TPU:0, one launch (start us, length us, event | category | flops | bytes accessed | tf_op | source)
XLA Modules:
  0.0 375.5 jit_solution(16419638537728177638)
XLA Ops:
  7.3 1.9 pad_maximum_fusion
  10.1 3.9 %collective-permute-start.5 = (f32[1,128,128]{2,1,0:T(8,128)S(1)}, f32[1,128,128]{2,1,0:T(8,128)S(1)}, u32[]{:S(2)}, u32[]{:S(2)}) collective-permute-start(f32[1,128,128]{2,1,0:T(8,128)S(1)} %get-tuple-element.66), channel_id=1, source_target_pairs={{0,1},{1,2},{2,3},{3,4},{4,5},{5,6},{6,7},{8,9},{9,10},{10,11},{11... | collective-permute-start | bytes 196616 | tf_op jit(solution)/shard_map/ppermute | solution.py:16
  14.0 1.3 collective-permute-start.4
  27.3 2.3 slice_bitcast_fusion
  29.6 56.8 %all-gather.2.cloned.1.call-done = f32[2,16,256,256]{3,2,1,0:T(8,128)} async-done(((f32[2,16,16,256]{3,2,1,0:T(8,128)}), f32[2,16,256,256]{3,2,1,0:T(8,128)}) %all-gather.2.cloned.1.call-update) | async-done | bytes 8388624 | tf_op jit(solution)/shard_map/all_gather | solution.py:61
  87.5 1.4 collective-permute-start
  88.9 4.5 %collective-permute-start.1 = (f32[1,128,128]{2,1,0:T(8,128)S(1)}, f32[1,128,128]{2,1,0:T(8,128)S(1)}, u32[]{:S(2)}, u32[]{:S(2)}) collective-permute-start(f32[1,128,128]{2,1,0:T(8,128)S(1)} %get-tuple-element.65), channel_id=1, source_target_pairs={{0,1},{1,2},{2,3},{3,4},{4,5},{5,6},{6,7},{8,9},{9,10},{10,11},{11... | collective-permute-start | bytes 196616 | tf_op jit(solution)/shard_map/ppermute | solution.py:16
  93.4 2.0 dynamic-slice_bitcast_fusion.1
  97.1 1.8 copy-done.30
  98.9 3.6 fusion.47
  103.3 3.5 collective-permute-start.7
  106.8 1.3 collective-permute-start.6
  108.1 2.0 fusion.7
  111.2 7.9 %gather_fusion.3 = f32[512]{0:T(512)} fusion(f32[262144]{0:T(1024)} %copy-done.9, s32[1024]{0:T(1024)S(1)} %pad_clamp_fusion), kind=kCustom, calls=%fused_computation.3 | custom fusion | bytes 6144 | tf_op jit(solution)/shard_map/gather | solution.py:100
  119.1 1.9 fusion.21
  121.3 4.8 %multiply_add_fusion.3 = (f32[16,128,128]{2,1,0:T(8,128)S(1)}, f32[16,128,128]{2,1,0:T(8,128)}) fusion(f32[16,128,128]{2,1,0:T(8,128)S(1)} %bitcast.114, f32[2,16,256,256]{3,2,1,0:T(8,128)} %all-gather.2.cloned.1.call-done, s32[]{:T(128)S(6)} %select_n.55, s32[]{:T(128)S(6)} %select_n.56, f32[1,2,16,128,128]{4,3,2,1,0:T(8,128)} %param.20, ...), kind=kLoop, calls=%fused_computation.128 | loop fusion | flops 2359296 | bytes 11534344 | tf_op jit(solution)/shard_map/add | solution.py:96
  127.0 4.4 %collective-permute-start.9 = (f32[1,128,128]{2,1,0:T(8,128)S(1)}, f32[1,128,128]{2,1,0:T(8,128)S(1)}, u32[]{:S(2)}, u32[]{:S(2)}) collective-permute-start(f32[1,128,128]{2,1,0:T(8,128)S(1)} %get-tuple-element.76), channel_id=1, source_target_pairs={{0,1},{1,2},{2,3},{3,4},{4,5},{5,6},{6,7},{8,9},{9,10},{10,11},{11... | collective-permute-start | bytes 196616 | tf_op jit(solution)/shard_map/ppermute | solution.py:16
  131.3 1.3 collective-permute-start.8
  132.6 2.0 fusion.9
  134.6 1.2 subtract_multiply_fusion.4
  135.8 8.0 %gather_fusion.2 = f32[512]{0:T(512)} fusion(f32[262144]{0:T(1024)} %copy-done.12, s32[1024]{0:T(1024)S(1)} %pad_clamp_fusion), kind=kCustom, calls=%fused_computation.2 | custom fusion | bytes 6144 | tf_op jit(solution)/shard_map/gather | solution.py:100
  143.8 1.9 fusion.22
  146.3 4.5 %multiply_add_fusion.2 = (f32[16,128,128]{2,1,0:T(8,128)S(1)}, f32[16,128,128]{2,1,0:T(8,128)}) fusion(f32[16,128,128]{2,1,0:T(8,128)S(1)} %bitcast.115, f32[16,128,128]{2,1,0:T(8,128)S(1)} %bitcast.120, f32[2,16,256,256]{3,2,1,0:T(8,128)} %all-gather.2.cloned.1.call-done, s32[]{:T(128)S(6)} %select_n.55, s32[]{:T(128)S(6)} %select_n.56, ...), kind=kLoop, calls=%fused_computation.127 | loop fusion | flops 2359296 | bytes 11534344 | tf_op jit(solution)/shard_map/add | solution.py:96
  151.6 4.4 %collective-permute-start.11 = (f32[1,128,128]{2,1,0:T(8,128)S(1)}, f32[1,128,128]{2,1,0:T(8,128)S(1)}, u32[]{:S(2)}, u32[]{:S(2)}) collective-permute-start(f32[1,128,128]{2,1,0:T(8,128)S(1)} %get-tuple-element.74), channel_id=1, source_target_pairs={{0,1},{1,2},{2,3},{3,4},{4,5},{5,6},{6,7},{8,9},{9,10},{10,11},{11... | collective-permute-start | bytes 196616 | tf_op jit(solution)/shard_map/ppermute | solution.py:16
  156.0 1.5 collective-permute-start.10
  157.5 2.0 fusion.11
  159.5 1.2 subtract_multiply_fusion.3
  160.7 7.9 %gather_fusion.1 = f32[512]{0:T(512)} fusion(f32[262144]{0:T(1024)} %copy-done.15, s32[1024]{0:T(1024)S(1)} %pad_clamp_fusion), kind=kCustom, calls=%fused_computation.1 | custom fusion | bytes 6144 | tf_op jit(solution)/shard_map/gather | solution.py:100
  168.6 1.9 fusion.23
  171.1 5.4 %multiply_add_fusion.1 = (f32[16,128,128]{2,1,0:T(8,128)}, f32[16,128,128]{2,1,0:T(8,128)}, f32[16,128,128]{2,1,0:T(8,128)S(1)}) fusion(f32[16,128,128]{2,1,0:T(8,128)S(1)} %bitcast.121, f32[16,128,128]{2,1,0:T(8,128)S(1)} %bitcast.126, f32[2,16,256,256]{3,2,1,0:T(8,128)} %all-gather.2.cloned.1.call-done, s32[]{:T(128)S(6)} %select_n.55, s32[]{:T(128)S(6)} %select_n.56, ...), kind=kLoop, calls=%fused_computation.126 | loop fusion | flops 2621440 | bytes 13631496 | tf_op jit(solution)/shard_map/add | solution.py:96
  176.5 1.3 subtract_multiply_fusion.7
  177.8 2.0 fusion.3
  179.8 2.1 fusion.55
  182.0 6.5 %gather_fusion = f32[512]{0:T(512)S(1)} fusion(f32[262144]{0:T(1024)} %fusion.55, s32[1024]{0:T(1024)S(1)} %pad_clamp_fusion), kind=kCustom, calls=%fused_computation | custom fusion | bytes 6144 | tf_op jit(solution)/shard_map/gather | solution.py:100
  188.4 5.0 %collective-permute-start.3 = (f32[1,128,128]{2,1,0:T(8,128)S(1)}, f32[1,128,128]{2,1,0:T(8,128)S(1)}, u32[]{:S(2)}, u32[]{:S(2)}) collective-permute-start(f32[1,128,128]{2,1,0:T(8,128)S(1)} %get-tuple-element.80), channel_id=1, source_target_pairs={{0,1},{1,2},{2,3},{3,4},{4,5},{5,6},{6,7},{8,9},{9,10},{10,11},{11... | collective-permute-start | bytes 196616 | tf_op jit(solution)/shard_map/ppermute | solution.py:16
  193.5 1.3 collective-permute-start.2
  195.3 5.0 %collective-permute-done.2 = f32[1,128,128]{2,1,0:T(8,128)S(1)} collective-permute-done((f32[1,128,128]{2,1,0:T(8,128)S(1)}, f32[1,128,128]{2,1,0:T(8,128)S(1)}, u32[]{:S(2)}, u32[]{:S(2)}) %collective-permute-start.2) | collective-permute-done | bytes 65568 | tf_op jit(solution)/shard_map/ppermute | solution.py:17
  200.4 1.8 fusion.19
  202.2 3.1 fusion.45
  205.3 5.2 %scatter_fusion = f32[262144]{0:T(1024)} fusion(f32[262144]{0:T(1024)} %bitcast.128, s32[512]{0:T(512)S(1)} %bitcast.149, f32[512]{0:T(512)S(1)} %get-tuple-element.91), kind=kCustom, calls=%fused_computation.4 | custom fusion | flops 512 | bytes 8192 | tf_op jit(solution)/shard_map/scatter-add | solution.py:37
  210.5 2.3 fusion.50
  213.5 4.8 %collective-permute-start.13 = (f32[1,128,128]{2,1,0:T(8,128)S(1)}, f32[1,128,128]{2,1,0:T(8,128)S(1)}, u32[]{:S(2)}, u32[]{:S(2)}) collective-permute-start(f32[1,128,128]{2,1,0:T(8,128)S(1)} %get-tuple-element.72), channel_id=1, source_target_pairs={{0,1},{1,2},{2,3},{3,4},{4,5},{5,6},{6,7},{8,9},{9,10},{10,11},{11... | collective-permute-start | bytes 196616 | tf_op jit(solution)/shard_map/ppermute | solution.py:16
  218.3 1.3 collective-permute-start.12
  220.2 4.3 %collective-permute-done.12 = f32[1,128,128]{2,1,0:T(8,128)S(1)} collective-permute-done((f32[1,128,128]{2,1,0:T(8,128)S(1)}, f32[1,128,128]{2,1,0:T(8,128)S(1)}, u32[]{:S(2)}, u32[]{:S(2)}) %collective-permute-start.12) | collective-permute-done | bytes 65568 | tf_op jit(solution)/shard_map/ppermute | solution.py:17
  224.6 1.5 fusion.34
  226.2 5.2 %scatter_fusion.1 = f32[262144]{0:T(1024)} fusion(f32[262144]{0:T(1024)} %bitcast.133, s32[512]{0:T(512)S(1)} %bitcast.150, f32[512]{0:T(512)S(1)} %get-tuple-element.90), kind=kCustom, calls=%fused_computation.5 | custom fusion | flops 512 | bytes 8192 | tf_op jit(solution)/shard_map/scatter-add | solution.py:37
  231.3 2.3 fusion.49
  234.3 2.8 collective-permute-start.15
  237.2 1.5 collective-permute-start.14
  239.0 4.3 %collective-permute-done.14 = f32[1,128,128]{2,1,0:T(8,128)S(1)} collective-permute-done((f32[1,128,128]{2,1,0:T(8,128)S(1)}, f32[1,128,128]{2,1,0:T(8,128)S(1)}, u32[]{:S(2)}, u32[]{:S(2)}) %collective-permute-start.14) | collective-permute-done | bytes 65568 | tf_op jit(solution)/shard_map/ppermute | solution.py:17
  243.5 1.5 fusion.31
  245.0 5.2 %scatter_fusion.2 = f32[262144]{0:T(1024)} fusion(f32[262144]{0:T(1024)} %bitcast.138, s32[512]{0:T(512)S(1)} %bitcast.151, f32[512]{0:T(512)S(1)} %get-tuple-element.89), kind=kCustom, calls=%fused_computation.6 | custom fusion | flops 512 | bytes 8192 | tf_op jit(solution)/shard_map/scatter-add | solution.py:37
  250.2 2.3 fusion.48
  253.2 4.8 %collective-permute-start.17 = (f32[1,128,128]{2,1,0:T(8,128)S(1)}, f32[1,128,128]{2,1,0:T(8,128)S(1)}, u32[]{:S(2)}, u32[]{:S(2)}) collective-permute-start(f32[1,128,128]{2,1,0:T(8,128)S(1)} %get-tuple-element.68), channel_id=1, source_target_pairs={{0,1},{1,2},{2,3},{3,4},{4,5},{5,6},{6,7},{8,9},{9,10},{10,11},{11... | collective-permute-start | bytes 196616 | tf_op jit(solution)/shard_map/ppermute | solution.py:16
  258.0 1.3 collective-permute-start.16
  259.9 4.3 %collective-permute-done.16 = f32[1,128,128]{2,1,0:T(8,128)S(1)} collective-permute-done((f32[1,128,128]{2,1,0:T(8,128)S(1)}, f32[1,128,128]{2,1,0:T(8,128)S(1)}, u32[]{:S(2)}, u32[]{:S(2)}) %collective-permute-start.16) | collective-permute-done | bytes 65568 | tf_op jit(solution)/shard_map/ppermute | solution.py:17
  264.3 1.6 fusion.28
  265.9 5.3 %scatter_fusion.3 = f32[262144]{0:T(1024)} fusion(f32[262144]{0:T(1024)} %bitcast.143, s32[512]{0:T(512)S(1)} %bitcast.152, f32[512]{0:T(512)S(1)} %get-tuple-element.88), kind=kCustom, calls=%fused_computation.7 | custom fusion | flops 512 | bytes 8192 | tf_op jit(solution)/shard_map/scatter-add | solution.py:37
  271.2 4.3 %multiply_add_fusion = f32[16,128,128]{2,1,0:T(8,128)} fusion(f32[16,128,128]{2,1,0:T(8,128)} %bitcast.144, f32[16,128,128]{2,1,0:T(8,128)} %get-tuple-element.58, f32[16,128,128]{2,1,0:T(8,128)S(1)} %bitcast.141, f32[16,128,128]{2,1,0:T(8,128)} %get-tuple-element.56, f32[16,128,128]{2,1,0:T(8,128)S(1)} %bitcast.137, f32[16,128,128]{2,1,0:T(8,128)} %get-tuple-element.54, ...), kind=kLoop, calls=%fused_computation.125 | loop fusion | flops 1835008 | bytes 9437184 | tf_op jit(solution)/shard_map/add | solution.py:111
  275.5 2.4 broadcast_in_dim.15
  277.9 13.9 %dynamic_update_slice.3 = f32[16,256,256]{2,1,0:T(8,128)} dynamic-update-slice(f32[16,256,256]{2,1,0:T(8,128)} %broadcast_in_dim.15, f32[16,128,128]{2,1,0:T(8,128)S(1)} %copy-done.33, s32[]{:T(128)} %constant.95.clone.1, s32[]{:T(128)S(6)} %select_n.55, s32[]{:T(128)S(6)} %select_n.56) | dynamic-update-slice | bytes 2097156 | tf_op jit(solution)/shard_map/dynamic_update_slice | solution.py:114
  291.8 1.2 copy-done.17
  293.0 3.9 %maximum_bitcast_fusion = (f32[1,2,16,128,128]{4,3,2,1,0:T(8,128)}, f32[1,2,16,128,128]{4,3,2,1,0:T(8,128)}) fusion(f32[1,16,128,128]{3,2,1,0:T(8,128)} %bitcast.54, f32[1,16,128,128]{3,2,1,0:T(8,128)S(1)} %bitcast.127, f32[1,16,128,128]{3,2,1,0:T(8,128)} %bitcast.145, f32[1,16,128,128]{3,2,1,0:T(8,128)S(1)} %bitcast.142), kind=kLoop, calls=%fused_computation.44 | loop fusion | flops 1048576 | bytes 8388608 | tf_op jit(solution)/shard_map/broadcast_in_dim | solution.py:120
  296.9 71.7 %reduce-scatter.2.cloned.1.call-done = f32[16,16,256]{2,1,0:T(8,128)} async-done(((f32[16,256,256]{2,1,0:T(8,128)}), f32[16,16,256]{2,1,0:T(8,128)}) %reduce-scatter.2.cloned.1.call-update) | async-done | bytes 262160 | tf_op jit(solution)/shard_map/reduce_scatter | solution.py:119
  (139 shorter events, 16.2 us)
Async XLA Ops:
  7.2 8.1 %copy-start = (s32[16,2]{0,1:T(2,128)S(1)}, s32[16,2]{0,1:T(2,128)}, u32[]{:S(2)}) copy-start(s32[16,2]{0,1:T(2,128)} %param.19) | copy-start | bytes 388
  7.2 11.3 %copy-start.42 = (s32[1,3]{1,0:T(1,128)S(1)}, s32[1,3]{1,0:T(1,128)}, u32[]{:S(2)}) copy-start(s32[1,3]{1,0:T(1,128)} %param.23) | copy-start | bytes 40
  7.2 14.5 %copy-start.35 = (f32[1,4]{1,0:T(1,128)S(1)}, f32[1,4]{1,0:T(1,128)}, u32[]{:S(2)}) copy-start(f32[1,4]{1,0:T(1,128)} %param.22) | copy-start | bytes 52
  7.2 17.7 %copy-start.41 = (s32[1,512,3]{1,0,2:T(1,128)S(1)}, s32[1,512,3]{1,0,2:T(1,128)}, u32[]{:S(2)}) copy-start(s32[1,512,3]{1,0,2:T(1,128)} %param.24) | copy-start | bytes 18436
  7.2 19.5 %copy-start.34 = (f32[1,4,512]{2,1,0:T(4,128)S(1)}, f32[1,4,512]{2,1,0:T(4,128)}, u32[]{:S(2)}) copy-start(f32[1,4,512]{2,1,0:T(4,128)} %param.25) | copy-start | bytes 24580
  7.2 79.1 %all-gather.2.cloned.1.call-start = ((), (), s32[]{:S(2)}) async-start(), calls=%async_computation.1 | async-start | bytes 8912896 | tf_op jit(solution)/shard_map/all_gather | solution.py:61
  9.2 359.5 %reduce-scatter.2.cloned.1.call-start = ((), (), s32[]{:S(2)}) async-start(), calls=%async_computation.2 | async-start | bytes 4456448 | tf_op jit(solution)/shard_map/reduce_scatter | solution.py:119
  10.1 86.8 %collective-permute-start.5 = (f32[1,128,128]{2,1,0:T(8,128)S(1)}, f32[1,128,128]{2,1,0:T(8,128)S(1)}, u32[]{:S(2)}, u32[]{:S(2)}) collective-permute-start(f32[1,128,128]{2,1,0:T(8,128)S(1)} %get-tuple-element.66), channel_id=1, source_target_pairs={{0,1},{1,2},{2,3},{3,4},{4,5},{5,6},{6,7},{8,9},{9,10},{10,11},{11... | collective-permute-start | bytes 196616 | tf_op jit(solution)/shard_map/ppermute | solution.py:16
  14.0 82.9 %collective-permute-start.4 = (f32[1,128,128]{2,1,0:T(8,128)S(1)}, f32[1,128,128]{2,1,0:T(8,128)S(1)}, u32[]{:S(2)}, u32[]{:S(2)}) collective-permute-start(f32[1,128,128]{2,1,0:T(8,128)S(1)} %get-tuple-element.67), channel_id=1, source_target_pairs={{1,0},{2,1},{3,2},{4,3},{5,4},{6,5},{7,6},{9,8},{10,9},{11,10},{12... | collective-permute-start | bytes 196616 | tf_op jit(solution)/shard_map/ppermute | solution.py:17
  87.4 8.0 %copy-start.25 = (f32[16,128,128]{2,1,0:T(8,128)S(1)}, f32[16,128,128]{2,1,0:T(8,128)}, u32[]{:S(2)}) copy-start(f32[16,128,128]{2,1,0:T(8,128)} %slice_bitcast_fusion) | copy-start | bytes 3145732
  87.5 9.5 %collective-permute-start = (f32[1,128,128]{2,1,0:T(8,128)S(1)}, f32[1,128,128]{2,1,0:T(8,128)S(1)}, u32[]{:S(2)}, u32[]{:S(2)}) collective-permute-start(f32[1,128,128]{2,1,0:T(8,128)S(1)} %get-tuple-element.64), channel_id=1, source_target_pairs={{1,0},{2,1},{3,2},{4,3},{5,4},{6,5},{7,6},{9,8},{10,9},{11,10},{12... | collective-permute-start | bytes 196616 | tf_op jit(solution)/shard_map/ppermute | solution.py:17
  88.9 8.1 %collective-permute-start.1 = (f32[1,128,128]{2,1,0:T(8,128)S(1)}, f32[1,128,128]{2,1,0:T(8,128)S(1)}, u32[]{:S(2)}, u32[]{:S(2)}) collective-permute-start(f32[1,128,128]{2,1,0:T(8,128)S(1)} %get-tuple-element.65), channel_id=1, source_target_pairs={{0,1},{1,2},{2,3},{3,4},{4,5},{5,6},{6,7},{8,9},{9,10},{10,11},{11... | collective-permute-start | bytes 196616 | tf_op jit(solution)/shard_map/ppermute | solution.py:16
  96.9 13.2 %copy-start.2 = (f32[16,129,128]{2,1,0:T(8,128)}, f32[16,129,128]{2,1,0:T(8,128)S(1)}, u32[]{:S(2)}) copy-start(f32[16,129,128]{2,1,0:T(8,128)S(1)} %get-tuple-element.60) | copy-start | bytes 3170308
  96.9 2.0 copy-start.30
  103.3 6.8 %copy-start.9 = (f32[262144]{0:T(1024)}, f32[262144]{0:T(1024)S(1)}, u32[]{:S(2)}) copy-start(f32[262144]{0:T(1024)S(1)} %fusion.52) | copy-start | bytes 3145732
  103.3 15.8 %collective-permute-start.7 = (f32[1,128,128]{2,1,0:T(8,128)S(1)}, f32[1,128,128]{2,1,0:T(8,128)S(1)}, u32[]{:S(2)}, u32[]{:S(2)}) collective-permute-start(f32[1,128,128]{2,1,0:T(8,128)S(1)} %get-tuple-element.78), channel_id=1, source_target_pairs={{0,1},{1,2},{2,3},{3,4},{4,5},{5,6},{6,7},{8,9},{9,10},{10,11},{11... | collective-permute-start | bytes 196616 | tf_op jit(solution)/shard_map/ppermute | solution.py:16
  106.8 12.3 %collective-permute-start.6 = (f32[1,128,128]{2,1,0:T(8,128)S(1)}, f32[1,128,128]{2,1,0:T(8,128)S(1)}, u32[]{:S(2)}, u32[]{:S(2)}) collective-permute-start(f32[1,128,128]{2,1,0:T(8,128)S(1)} %get-tuple-element.79), channel_id=1, source_target_pairs={{1,0},{2,1},{3,2},{4,3},{5,4},{6,5},{7,6},{9,8},{10,9},{11,10},{12... | collective-permute-start | bytes 196616 | tf_op jit(solution)/shard_map/ppermute | solution.py:17
  119.1 2.0 copy-start.10
  119.1 2.2 copy-start.29
  126.9 7.7 %copy-start.12 = (f32[262144]{0:T(1024)}, f32[262144]{0:T(1024)S(1)}, u32[]{:S(2)}) copy-start(f32[262144]{0:T(1024)S(1)} %fusion.53) | copy-start | bytes 3145732
  127.0 16.8 %collective-permute-start.9 = (f32[1,128,128]{2,1,0:T(8,128)S(1)}, f32[1,128,128]{2,1,0:T(8,128)S(1)}, u32[]{:S(2)}, u32[]{:S(2)}) collective-permute-start(f32[1,128,128]{2,1,0:T(8,128)S(1)} %get-tuple-element.76), channel_id=1, source_target_pairs={{0,1},{1,2},{2,3},{3,4},{4,5},{5,6},{6,7},{8,9},{9,10},{10,11},{11... | collective-permute-start | bytes 196616 | tf_op jit(solution)/shard_map/ppermute | solution.py:16
  131.3 12.4 %collective-permute-start.8 = (f32[1,128,128]{2,1,0:T(8,128)S(1)}, f32[1,128,128]{2,1,0:T(8,128)S(1)}, u32[]{:S(2)}, u32[]{:S(2)}) collective-permute-start(f32[1,128,128]{2,1,0:T(8,128)S(1)} %get-tuple-element.77), channel_id=1, source_target_pairs={{1,0},{2,1},{3,2},{4,3},{5,4},{6,5},{7,6},{9,8},{10,9},{11,10},{12... | collective-permute-start | bytes 196616 | tf_op jit(solution)/shard_map/ppermute | solution.py:17
  132.6 2.0 copy-start.3
  143.8 2.0 copy-start.11
  143.8 2.2 copy-start.13
  143.8 2.5 copy-start.28
  151.6 7.9 %copy-start.15 = (f32[262144]{0:T(1024)}, f32[262144]{0:T(1024)S(1)}, u32[]{:S(2)}) copy-start(f32[262144]{0:T(1024)S(1)} %fusion.54) | copy-start | bytes 3145732
  151.6 17.0 %collective-permute-start.11 = (f32[1,128,128]{2,1,0:T(8,128)S(1)}, f32[1,128,128]{2,1,0:T(8,128)S(1)}, u32[]{:S(2)}, u32[]{:S(2)}) collective-permute-start(f32[1,128,128]{2,1,0:T(8,128)S(1)} %get-tuple-element.74), channel_id=1, source_target_pairs={{0,1},{1,2},{2,3},{3,4},{4,5},{5,6},{6,7},{8,9},{9,10},{10,11},{11... | collective-permute-start | bytes 196616 | tf_op jit(solution)/shard_map/ppermute | solution.py:16
  156.0 12.6 %collective-permute-start.10 = (f32[1,128,128]{2,1,0:T(8,128)S(1)}, f32[1,128,128]{2,1,0:T(8,128)S(1)}, u32[]{:S(2)}, u32[]{:S(2)}) collective-permute-start(f32[1,128,128]{2,1,0:T(8,128)S(1)} %get-tuple-element.75), channel_id=1, source_target_pairs={{1,0},{2,1},{3,2},{4,3},{5,4},{6,5},{7,6},{9,8},{10,9},{11,10},{12... | collective-permute-start | bytes 196616 | tf_op jit(solution)/shard_map/ppermute | solution.py:17
  157.5 2.0 copy-start.4
  168.6 2.0 copy-start.14
  168.6 2.2 copy-start.16
  168.6 2.5 copy-start.27
  171.1 5.4 %copy-start.5 = (f32[16,129,128]{2,1,0:T(8,128)S(1)}, f32[16,129,128]{2,1,0:T(8,128)}, u32[]{:S(2)}) copy-start(f32[16,129,128]{2,1,0:T(8,128)} %copy-done.2) | copy-start | bytes 3170308
  176.5 1.3 copy-start.24
  179.8 15.0 %copy-start.36 = (f32[1,1,512]{2,1,0:T(1,128)S(1)}, f32[1,1,512]{2,1,0:T(1,128)}, u32[]{:S(2)}) copy-start(f32[1,1,512]{2,1,0:T(1,128)} %get-tuple-element.84) | copy-start | bytes 6148
  179.8 15.0 %copy-start.37 = (f32[1,1,512]{2,1,0:T(1,128)S(1)}, f32[1,1,512]{2,1,0:T(1,128)}, u32[]{:S(2)}) copy-start(f32[1,1,512]{2,1,0:T(1,128)} %get-tuple-element.85) | copy-start | bytes 6148
  179.8 15.0 %copy-start.38 = (f32[512]{0:T(512)S(1)}, f32[512]{0:T(512)}, u32[]{:S(2)}) copy-start(f32[512]{0:T(512)} %gather_fusion.3) | copy-start | bytes 6148
  179.8 15.0 %copy-start.39 = (f32[512]{0:T(512)S(1)}, f32[512]{0:T(512)}, u32[]{:S(2)}) copy-start(f32[512]{0:T(512)} %gather_fusion.2) | copy-start | bytes 6148
  179.8 15.0 %copy-start.40 = (f32[512]{0:T(512)S(1)}, f32[512]{0:T(512)}, u32[]{:S(2)}) copy-start(f32[512]{0:T(512)} %gather_fusion.1) | copy-start | bytes 6148
  179.8 15.0 %copy-start.43 = (pred[512]{0:T(512)(128)(4,1)S(1)}, pred[512]{0:T(512)(128)(4,1)}, u32[]{:S(2)}) copy-start(pred[512]{0:T(512)(128)(4,1)} %and_reduce_fusion) | copy-start | bytes 1540
  188.4 6.9 %collective-permute-start.3 = (f32[1,128,128]{2,1,0:T(8,128)S(1)}, f32[1,128,128]{2,1,0:T(8,128)S(1)}, u32[]{:S(2)}, u32[]{:S(2)}) collective-permute-start(f32[1,128,128]{2,1,0:T(8,128)S(1)} %get-tuple-element.80), channel_id=1, source_target_pairs={{0,1},{1,2},{2,3},{3,4},{4,5},{5,6},{6,7},{8,9},{9,10},{10,11},{11... | collective-permute-start | bytes 196616 | tf_op jit(solution)/shard_map/ppermute | solution.py:16
  193.5 6.9 %collective-permute-start.2 = (f32[1,128,128]{2,1,0:T(8,128)S(1)}, f32[1,128,128]{2,1,0:T(8,128)S(1)}, u32[]{:S(2)}, u32[]{:S(2)}) collective-permute-start(f32[1,128,128]{2,1,0:T(8,128)S(1)} %get-tuple-element.81), channel_id=1, source_target_pairs={{1,0},{2,1},{3,2},{4,3},{5,4},{6,5},{7,6},{9,8},{10,9},{11,10},{12... | collective-permute-start | bytes 196616 | tf_op jit(solution)/shard_map/ppermute | solution.py:17
  194.8 7.3 %copy-start.26 = (f32[16,129,128]{2,1,0:T(8,128)S(1)}, f32[16,129,128]{2,1,0:T(8,128)}, u32[]{:S(2)}) copy-start(f32[16,129,128]{2,1,0:T(8,128)} %subtract_multiply_fusion.7) | copy-start | bytes 3170308
  194.9 7.3 %copy-start.31 = (f32[16,128,129]{2,1,0:T(8,128)S(1)}, f32[16,128,129]{2,1,0:T(8,128)}, u32[]{:S(2)}) copy-start(f32[16,128,129]{2,1,0:T(8,128)} %fusion.3) | copy-start | bytes 3170308
  212.8 6.8 %copy-start.6 = (f32[16,129,128]{2,1,0:T(8,128)S(1)}, f32[16,129,128]{2,1,0:T(8,128)}, u32[]{:S(2)}) copy-start(f32[16,129,128]{2,1,0:T(8,128)} %copy-done.2) | copy-start | bytes 3170308
  213.5 6.7 %collective-permute-start.13 = (f32[1,128,128]{2,1,0:T(8,128)S(1)}, f32[1,128,128]{2,1,0:T(8,128)S(1)}, u32[]{:S(2)}, u32[]{:S(2)}) collective-permute-start(f32[1,128,128]{2,1,0:T(8,128)S(1)} %get-tuple-element.72), channel_id=1, source_target_pairs={{0,1},{1,2},{2,3},{3,4},{4,5},{5,6},{6,7},{8,9},{9,10},{10,11},{11... | collective-permute-start | bytes 196616 | tf_op jit(solution)/shard_map/ppermute | solution.py:16
  218.3 6.2 %collective-permute-start.12 = (f32[1,128,128]{2,1,0:T(8,128)S(1)}, f32[1,128,128]{2,1,0:T(8,128)S(1)}, u32[]{:S(2)}, u32[]{:S(2)}) collective-permute-start(f32[1,128,128]{2,1,0:T(8,128)S(1)} %get-tuple-element.73), channel_id=1, source_target_pairs={{1,0},{2,1},{3,2},{4,3},{5,4},{6,5},{7,6},{9,8},{10,9},{11,10},{12... | collective-permute-start | bytes 196616 | tf_op jit(solution)/shard_map/ppermute | solution.py:17
  219.8 4.9 %copy-start.18 = (f32[262144]{0:T(1024)S(1)}, f32[262144]{0:T(1024)}, u32[]{:S(2)}) copy-start(f32[262144]{0:T(1024)} %scatter_fusion) | copy-start | bytes 3145732
  219.8 4.9 %copy-start.32 = (f32[1,2,16,128,128]{4,3,2,1,0:T(8,128)S(1)}, f32[1,2,16,128,128]{4,3,2,1,0:T(8,128)}, u32[]{:S(2)}) copy-start(f32[1,2,16,128,128]{4,3,2,1,0:T(8,128)} %param.21) | copy-start | bytes 6291460
  233.7 5.0 %copy-start.7 = (f32[16,129,128]{2,1,0:T(8,128)S(1)}, f32[16,129,128]{2,1,0:T(8,128)}, u32[]{:S(2)}) copy-start(f32[16,129,128]{2,1,0:T(8,128)} %copy-done.2) | copy-start | bytes 3170308
  234.3 4.7 %collective-permute-start.15 = (f32[1,128,128]{2,1,0:T(8,128)S(1)}, f32[1,128,128]{2,1,0:T(8,128)S(1)}, u32[]{:S(2)}, u32[]{:S(2)}) collective-permute-start(f32[1,128,128]{2,1,0:T(8,128)S(1)} %get-tuple-element.70), channel_id=1, source_target_pairs={{0,1},{1,2},{2,3},{3,4},{4,5},{5,6},{6,7},{8,9},{9,10},{10,11},{11... | collective-permute-start | bytes 196616 | tf_op jit(solution)/shard_map/ppermute | solution.py:16
  237.2 6.2 %collective-permute-start.14 = (f32[1,128,128]{2,1,0:T(8,128)S(1)}, f32[1,128,128]{2,1,0:T(8,128)S(1)}, u32[]{:S(2)}, u32[]{:S(2)}) collective-permute-start(f32[1,128,128]{2,1,0:T(8,128)S(1)} %get-tuple-element.71), channel_id=1, source_target_pairs={{1,0},{2,1},{3,2},{4,3},{5,4},{6,5},{7,6},{9,8},{10,9},{11,10},{12... | collective-permute-start | bytes 196616 | tf_op jit(solution)/shard_map/ppermute | solution.py:17
  238.8 4.6 %copy-start.19 = (f32[262144]{0:T(1024)S(1)}, f32[262144]{0:T(1024)}, u32[]{:S(2)}) copy-start(f32[262144]{0:T(1024)} %scatter_fusion) | copy-start | bytes 3145732
  238.9 4.6 %copy-start.21 = (f32[262144]{0:T(1024)S(1)}, f32[262144]{0:T(1024)}, u32[]{:S(2)}) copy-start(f32[262144]{0:T(1024)} %scatter_fusion.1) | copy-start | bytes 3145732
  252.5 6.8 %copy-start.8 = (f32[16,129,128]{2,1,0:T(8,128)S(1)}, f32[16,129,128]{2,1,0:T(8,128)}, u32[]{:S(2)}) copy-start(f32[16,129,128]{2,1,0:T(8,128)} %copy-done.2) | copy-start | bytes 3170308
  253.2 6.7 %collective-permute-start.17 = (f32[1,128,128]{2,1,0:T(8,128)S(1)}, f32[1,128,128]{2,1,0:T(8,128)S(1)}, u32[]{:S(2)}, u32[]{:S(2)}) collective-permute-start(f32[1,128,128]{2,1,0:T(8,128)S(1)} %get-tuple-element.68), channel_id=1, source_target_pairs={{0,1},{1,2},{2,3},{3,4},{4,5},{5,6},{6,7},{8,9},{9,10},{10,11},{11... | collective-permute-start | bytes 196616 | tf_op jit(solution)/shard_map/ppermute | solution.py:16
  258.0 6.2 %collective-permute-start.16 = (f32[1,128,128]{2,1,0:T(8,128)S(1)}, f32[1,128,128]{2,1,0:T(8,128)S(1)}, u32[]{:S(2)}, u32[]{:S(2)}) collective-permute-start(f32[1,128,128]{2,1,0:T(8,128)S(1)} %get-tuple-element.69), channel_id=1, source_target_pairs={{1,0},{2,1},{3,2},{4,3},{5,4},{6,5},{7,6},{9,8},{10,9},{11,10},{12... | collective-permute-start | bytes 196616 | tf_op jit(solution)/shard_map/ppermute | solution.py:17
  259.4 4.9 %copy-start.22 = (f32[262144]{0:T(1024)S(1)}, f32[262144]{0:T(1024)}, u32[]{:S(2)}) copy-start(f32[262144]{0:T(1024)} %scatter_fusion.1) | copy-start | bytes 3145732
  259.5 4.9 %copy-start.23 = (f32[262144]{0:T(1024)S(1)}, f32[262144]{0:T(1024)}, u32[]{:S(2)}) copy-start(f32[262144]{0:T(1024)} %scatter_fusion.2) | copy-start | bytes 3145732
  265.9 5.3 %copy-start.20 = (f32[262144]{0:T(1024)S(1)}, f32[262144]{0:T(1024)}, u32[]{:S(2)}) copy-start(f32[262144]{0:T(1024)} %scatter_fusion) | copy-start | bytes 3145732
  275.5 2.4 copy-start.33
  291.8 1.2 copy-start.17
  293.0 75.6 %copy-start.1 = (s32[16,2]{0,1:T(2,128)S(1)}, s32[16,2]{0,1:T(2,128)}, u32[]{:S(2)}) copy-start(s32[16,2]{0,1:T(2,128)} %param.19) | copy-start | bytes 388
Sparse Core Ops, SparseCore 0:
  11.1 75.2 all-gather.1
  291.9 76.6 reduce-scatter.1
where the time goes:
time: 378 us; the launch traced here: 375 us
  waiting for transfers between devices  148 us (39%)
  other arithmetic  93.7 us (25%)
  local copies, waits for them, and re-layouts  59.9 us (16%)
  starting transfers between devices  50.4 us (13%)
  between operations  23.8 us (6%)
    reduce_scatter x1, waiting for transfers between devices, shards(): lax.psum_scatter(embedded, 'shot', scatter_dimension=1, tiled=True)  71.7 us
    all_gather x1, waiting for transfers between devices, shards(): gathered = lax.all_gather(stacked, 'shot', axis=2, tiled=True)  56.8 us
    ppermute x9, starting transfers between devices, with_halo(): before = lax.ppermute(last, axis, up)  38.2 us
    gather x4, local copies, waits for them, and re-layouts, shards(): sampled = following.reshape(-1)[receiver_flat]  30.3 us
    scatter-add x8, other arithmetic, add_cells(): return field.reshape(-1).at[positions].add(amounts).reshape(shape)  25.4 us
    add x4, other arithmetic, shards(): following = 2.0 * current - before + kappa_window * spread  18.3 us
    ppermute x9, waiting for transfers between devices, with_halo(): after = lax.ppermute(first, axis, down)  17.8 us
    dynamic_update_slice x1, local copies, waits for them, and re-layouts, shards(): lax.dynamic_update_slice(jnp.zeros((depth_cells, own_rows * groups, model...  13.9 us
  transfers between devices with their start and end apart: 20, of which 10 were waited for; matrix products, arithmetic and copies ran while one was open for 13% of the time, Pallas kernels for 0%

commit v1 on v0

--- a/solution.py
+++ b/solution.py
@@ -58,7 +58,9 @@
     row_anchor = anchor[0]
     col_anchor = anchor[1]
     stacked = jnp.stack([kappa, buoyancy])
-    gathered = lax.all_gather(stacked, "shot", axis=2, tiled=True)
+    gathered = jnp.concatenate(
+        lax.all_to_all(jnp.stack([stacked] * lax.axis_size("shot")), "shot", 0, 0), axis=2
+    )
     window = lax.dynamic_slice(
         gathered,
         (row_anchor * 0, row_anchor * 0, row_anchor, col_anchor),

time: 378 us -> 430 us (1.14)
  waiting for transfers between devices: 148 us -> 180 us
  starting transfers between devices: 50.4 us -> 69.1 us
    all_to_all x0 -> x1, waiting for transfers between devices: none -> 91.4 us  [shards(): lax.all_to_all(jnp.stack([stacked] * lax.axis_size('shot')), 'shot', 0, 0)]
    all_gather x1 -> x0, waiting for transfers between devices: 56.8 us -> none  [shards(): gathered = lax.all_gather(stacked, 'shot', axis=2, tiled=True)]
    ppermute x9, waiting for transfers between devices: 17.8 us -> 0.44 us  [with_halo(): after = lax.ppermute(first, axis, down)]
    ppermute x9, starting transfers between devices: 38.2 us -> 49.2 us  [with_halo(): before = lax.ppermute(last, axis, up)]
    reduce_scatter x1, waiting for transfers between devices: 71.7 us -> 81.1 us  [shards(): lax.psum_scatter(embedded, 'shot', scatter_dimension=1, tiled=True)]
    all_to_all x0 -> x1, starting transfers between devices: none -> 8.13 us  [shards(): lax.all_to_all(jnp.stack([stacked] * lax.axis_size('shot')), 'shot', 0, 0)]
    ppermute x9, waiting for transfers between devices: 1.45 us -> 6.82 us  [with_halo(): before = lax.ppermute(last, axis, up)]
    all_to_all x0 -> x1, local copies, waits for them, and re-layouts: none -> 4.37 us  [shards(): lax.all_to_all(jnp.stack([stacked] * lax.axis_size('shot')), 'shot', 0, 0)]
  transfers between devices with their start and end apart: 20 -> 20, of which waited for: 10 -> 10; matrix products, arithmetic and copies ran while one was open for 13% -> 11% of each run, Pallas kernels for 0% -> 0%
where the time goes in v1:
time: 430 us; the launch traced here: 427 us
  waiting for transfers between devices  180 us (42%)
  other arithmetic  91.4 us (21%)
  starting transfers between devices  69.1 us (16%)
  local copies, waits for them, and re-layouts  63.3 us (15%)
  between operations  23.8 us (6%)
    all_to_all x1, waiting for transfers between devices, shards(): lax.all_to_all(jnp.stack([stacked] * lax.axis_size('shot')), 'shot', 0, 0)  91.4 us
    reduce_scatter x1, waiting for transfers between devices, shards(): lax.psum_scatter(embedded, 'shot', scatter_dimension=1, tiled=True)  81.1 us
    ppermute x9, starting transfers between devices, with_halo(): before = lax.ppermute(last, axis, up)  49.2 us
    gather x4, local copies, waits for them, and re-layouts, shards(): sampled = following.reshape(-1)[receiver_flat]  30.4 us
    scatter-add x8, other arithmetic, add_cells(): return field.reshape(-1).at[positions].add(amounts).reshape(shape)  25.6 us
    add x4, other arithmetic, shards(): following = 2.0 * current - before + kappa_window * spread  16.3 us
    dynamic_update_slice x1, local copies, waits for them, and re-layouts, shards(): lax.dynamic_update_slice(jnp.zeros((depth_cells, own_rows * groups, model...  13.9 us
    ppermute x9, starting transfers between devices, with_halo(): after = lax.ppermute(first, axis, down)  11.8 us
  transfers between devices with their start and end apart: 20, of which 10 were waited for; matrix products, arithmetic and copies ran while one was open for 11% of the time, Pallas kernels for 0%

profile of v1, /device:TPU:0, one launch (start us, length us, event | category | flops | bytes accessed | tf_op | source)
XLA Modules:
  0.0 427.3 jit_solution(1192916603539917368)
XLA Ops:
  8.3 4.4 %stack.15 = f32[16,2,16,16,256]{4,3,2,1,0:T(8,128)} broadcast(f32[2,16,16,256]{3,2,1,0:T(8,128)S(1)} %pad_maximum_fusion), dimensions={1,2,3,4} | broadcast | bytes 8912896 | tf_op jit(solution)/shard_map/stack | solution.py:62
  12.6 8.1 %all-to-all-start = ((f32[16,2,16,16,256]{4,3,2,1,0:T(8,128)}), f32[16,2,16,16,256]{4,3,2,1,0:T(8,128)}, u32[]{:S(2)}, u32[]{:S(2)}) async-start(f32[16,2,16,16,256]{4,3,2,1,0:T(8,128)} %stack.15), calls=%async_computation | async-start | bytes 16777216 | tf_op jit(solution)/shard_map/all_to_all | solution.py:62
  20.8 1.3 collective-permute-start.4
  22.1 4.5 %collective-permute-start.5 = (f32[1,128,128]{2,1,0:T(8,128)S(1)}, f32[1,128,128]{2,1,0:T(8,128)S(1)}, u32[]{:S(2)}, u32[]{:S(2)}) collective-permute-start(f32[1,128,128]{2,1,0:T(8,128)S(1)} %get-tuple-element.66), channel_id=1, source_target_pairs={{0,1},{1,2},{2,3},{3,4},{4,5},{5,6},{6,7},{8,9},{9,10},{10,11},{11... | collective-permute-start | bytes 196616 | tf_op jit(solution)/shard_map/ppermute | solution.py:16
  39.9 91.4 %all-to-all-done = f32[16,2,16,16,256]{4,3,2,1,0:T(8,128)} async-done(((f32[16,2,16,16,256]{4,3,2,1,0:T(8,128)}), f32[16,2,16,16,256]{4,3,2,1,0:T(8,128)}, u32[]{:S(2)}, u32[]{:S(2)}) %all-to-all-start) | async-done | bytes 8388640 | tf_op jit(solution)/shard_map/all_to_all | solution.py:62
  131.2 4.4 %copy.12 = f32[16,2,16,16,256]{4,3,0,2,1:T(8,128)S(1)} copy(f32[16,2,16,16,256]{4,3,2,1,0:T(8,128)} %all-to-all-done) | data formatting | bytes 16777216 | tf_op jit(solution)/shard_map/all_to_all | solution.py:62
  136.1 1.4 collective-permute-start
  137.5 6.1 %collective-permute-start.1 = (f32[1,128,128]{2,1,0:T(8,128)S(1)}, f32[1,128,128]{2,1,0:T(8,128)S(1)}, u32[]{:S(2)}, u32[]{:S(2)}) collective-permute-start(f32[1,128,128]{2,1,0:T(8,128)S(1)} %get-tuple-element.65), channel_id=1, source_target_pairs={{0,1},{1,2},{2,3},{3,4},{4,5},{5,6},{6,7},{8,9},{9,10},{10,11},{11... | collective-permute-start | bytes 196616 | tf_op jit(solution)/shard_map/ppermute | solution.py:16
  143.7 1.2 fusion.5
  147.1 1.9 fusion.47
  149.9 1.3 collective-permute-start.6
  151.2 5.4 %collective-permute-start.7 = (f32[1,128,128]{2,1,0:T(8,128)S(1)}, f32[1,128,128]{2,1,0:T(8,128)S(1)}, u32[]{:S(2)}, u32[]{:S(2)}) collective-permute-start(f32[1,128,128]{2,1,0:T(8,128)S(1)} %get-tuple-element.78), channel_id=1, source_target_pairs={{0,1},{1,2},{2,3},{3,4},{4,5},{5,6},{6,7},{8,9},{9,10},{10,11},{11... | collective-permute-start | bytes 196616 | tf_op jit(solution)/shard_map/ppermute | solution.py:16
  156.7 2.0 fusion.7
  159.8 7.9 %gather_fusion.3 = f32[512]{0:T(512)} fusion(f32[262144]{0:T(1024)} %copy-done.9, s32[1024]{0:T(1024)S(1)} %pad_clamp_fusion), kind=kCustom, calls=%fused_computation.3 | custom fusion | bytes 6144 | tf_op jit(solution)/shard_map/gather | solution.py:102
  167.8 2.0 fusion.21
  169.9 4.8 %multiply_add_fusion.3 = (f32[16,128,128]{2,1,0:T(8,128)S(1)}, f32[16,128,128]{2,1,0:T(8,128)}) fusion(f32[16,128,128]{2,1,0:T(8,128)S(1)} %bitcast.117, f32[2,16,256,256]{3,2,1,0:T(8,128)} %bitcast.149, s32[]{:T(128)S(6)} %select_n.55, s32[]{:T(128)S(6)} %select_n.56, f32[1,2,16,128,128]{4,3,2,1,0:T(8,128)} %param.20, f32[16,128,129]{2,1,0:T(8,128)} %fusion.7, ...), kind=kLoop, calls=%fused_computation.128 | loop fusion | flops 2359296 | bytes 11534344 | tf_op jit(solution)/shard_map/add | solution.py:98
  175.6 1.3 collective-permute-start.8
  176.9 5.3 %collective-permute-start.9 = (f32[1,128,128]{2,1,0:T(8,128)S(1)}, f32[1,128,128]{2,1,0:T(8,128)S(1)}, u32[]{:S(2)}, u32[]{:S(2)}) collective-permute-start(f32[1,128,128]{2,1,0:T(8,128)S(1)} %get-tuple-element.76), channel_id=1, source_target_pairs={{0,1},{1,2},{2,3},{3,4},{4,5},{5,6},{6,7},{8,9},{9,10},{10,11},{11... | collective-permute-start | bytes 196616 | tf_op jit(solution)/shard_map/ppermute | solution.py:16
  182.2 2.0 fusion.9
  184.2 1.2 subtract_multiply_fusion.4
  185.4 7.8 %gather_fusion.2 = f32[512]{0:T(512)} fusion(f32[262144]{0:T(1024)} %copy-done.12, s32[1024]{0:T(1024)S(1)} %pad_clamp_fusion), kind=kCustom, calls=%fused_computation.2 | custom fusion | bytes 6144 | tf_op jit(solution)/shard_map/gather | solution.py:102
  193.2 2.0 fusion.22
  195.7 4.5 %multiply_add_fusion.2 = (f32[16,128,128]{2,1,0:T(8,128)S(1)}, f32[16,128,128]{2,1,0:T(8,128)}) fusion(f32[16,128,128]{2,1,0:T(8,128)S(1)} %bitcast.118, f32[16,128,128]{2,1,0:T(8,128)S(1)} %bitcast.123, f32[2,16,256,256]{3,2,1,0:T(8,128)} %bitcast.150, s32[]{:T(128)S(6)} %select_n.55, s32[]{:T(128)S(6)} %select_n.56, f32[16,128,129]{2,1,0:T(8,128)} %fusion.9, ...), kind=kLoop, calls=%fused_computation.127 | loop fusion | flops 2359296 | bytes 11534344 | tf_op jit(solution)/shard_map/add | solution.py:98
  201.1 1.3 collective-permute-start.10
  202.4 5.4 %collective-permute-start.11 = (f32[1,128,128]{2,1,0:T(8,128)S(1)}, f32[1,128,128]{2,1,0:T(8,128)S(1)}, u32[]{:S(2)}, u32[]{:S(2)}) collective-permute-start(f32[1,128,128]{2,1,0:T(8,128)S(1)} %get-tuple-element.74), channel_id=1, source_target_pairs={{0,1},{1,2},{2,3},{3,4},{4,5},{5,6},{6,7},{8,9},{9,10},{10,11},{11... | collective-permute-start | bytes 196616 | tf_op jit(solution)/shard_map/ppermute | solution.py:16
  207.8 2.0 fusion.11
  209.8 1.2 subtract_multiply_fusion.3
  210.9 7.9 %gather_fusion.1 = f32[512]{0:T(512)} fusion(f32[262144]{0:T(1024)} %copy-done.15, s32[1024]{0:T(1024)S(1)} %pad_clamp_fusion), kind=kCustom, calls=%fused_computation.1 | custom fusion | bytes 6144 | tf_op jit(solution)/shard_map/gather | solution.py:102
  218.9 2.0 fusion.23
  221.4 5.1 %multiply_add_fusion.1 = (f32[16,128,128]{2,1,0:T(8,128)}, f32[16,128,128]{2,1,0:T(8,128)}, f32[16,128,128]{2,1,0:T(8,128)S(1)}) fusion(f32[16,128,128]{2,1,0:T(8,128)S(1)} %bitcast.124, f32[16,128,128]{2,1,0:T(8,128)S(1)} %bitcast.129, f32[2,16,256,256]{3,2,1,0:T(8,128)} %bitcast.151, s32[]{:T(128)S(6)} %select_n.55, s32[]{:T(128)S(6)} %select_n.56, ...), kind=kLoop, calls=%fused_computation.126 | loop fusion | flops 2621440 | bytes 13631496 | tf_op jit(solution)/shard_map/add | solution.py:98
  226.5 1.3 subtract_multiply_fusion.7
  227.8 2.0 fusion.3
  229.8 2.2 fusion.55
  232.0 6.7 %gather_fusion = f32[512]{0:T(512)S(1)} fusion(f32[262144]{0:T(1024)} %fusion.55, s32[1024]{0:T(1024)S(1)} %pad_clamp_fusion), kind=kCustom, calls=%fused_computation | custom fusion | bytes 6144 | tf_op jit(solution)/shard_map/gather | solution.py:102
  238.7 1.3 collective-permute-start.2
  240.0 5.1 %collective-permute-start.3 = (f32[1,128,128]{2,1,0:T(8,128)S(1)}, f32[1,128,128]{2,1,0:T(8,128)S(1)}, u32[]{:S(2)}, u32[]{:S(2)}) collective-permute-start(f32[1,128,128]{2,1,0:T(8,128)S(1)} %get-tuple-element.80), channel_id=1, source_target_pairs={{0,1},{1,2},{2,3},{3,4},{4,5},{5,6},{6,7},{8,9},{9,10},{10,11},{11... | collective-permute-start | bytes 196616 | tf_op jit(solution)/shard_map/ppermute | solution.py:16
  245.5 1.6 collective-permute-done.3
  247.1 1.9 fusion.19
  249.0 3.0 fusion.45
  251.9 5.2 %scatter_fusion = f32[262144]{0:T(1024)} fusion(f32[262144]{0:T(1024)} %bitcast.131, s32[512]{0:T(512)S(1)} %bitcast.161, f32[512]{0:T(512)S(1)} %get-tuple-element.91), kind=kCustom, calls=%fused_computation.4 | custom fusion | flops 512 | bytes 8192 | tf_op jit(solution)/shard_map/scatter-add | solution.py:37
  257.1 2.3 fusion.50
  260.1 1.3 collective-permute-start.12
  261.4 5.4 %collective-permute-start.13 = (f32[1,128,128]{2,1,0:T(8,128)S(1)}, f32[1,128,128]{2,1,0:T(8,128)S(1)}, u32[]{:S(2)}, u32[]{:S(2)}) collective-permute-start(f32[1,128,128]{2,1,0:T(8,128)S(1)} %get-tuple-element.72), channel_id=1, source_target_pairs={{0,1},{1,2},{2,3},{3,4},{4,5},{5,6},{6,7},{8,9},{9,10},{10,11},{11... | collective-permute-start | bytes 196616 | tf_op jit(solution)/shard_map/ppermute | solution.py:16
  267.2 1.6 collective-permute-done.13
  269.0 1.5 fusion.34
  270.4 5.2 %scatter_fusion.1 = f32[262144]{0:T(1024)} fusion(f32[262144]{0:T(1024)} %bitcast.136, s32[512]{0:T(512)S(1)} %bitcast.162, f32[512]{0:T(512)S(1)} %get-tuple-element.90), kind=kCustom, calls=%fused_computation.5 | custom fusion | flops 512 | bytes 8192 | tf_op jit(solution)/shard_map/scatter-add | solution.py:37
  275.6 2.3 fusion.49
  278.6 1.3 collective-permute-start.14
  279.9 6.0 %collective-permute-start.15 = (f32[1,128,128]{2,1,0:T(8,128)S(1)}, f32[1,128,128]{2,1,0:T(8,128)S(1)}, u32[]{:S(2)}, u32[]{:S(2)}) collective-permute-start(f32[1,128,128]{2,1,0:T(8,128)S(1)} %get-tuple-element.70), channel_id=1, source_target_pairs={{0,1},{1,2},{2,3},{3,4},{4,5},{5,6},{6,7},{8,9},{9,10},{10,11},{11... | collective-permute-start | bytes 196616 | tf_op jit(solution)/shard_map/ppermute | solution.py:16
  286.1 1.5 collective-permute-done.15
  287.8 1.5 fusion.31
  289.3 5.2 %scatter_fusion.2 = f32[262144]{0:T(1024)} fusion(f32[262144]{0:T(1024)} %bitcast.141, s32[512]{0:T(512)S(1)} %bitcast.163, f32[512]{0:T(512)S(1)} %get-tuple-element.89), kind=kCustom, calls=%fused_computation.6 | custom fusion | flops 512 | bytes 8192 | tf_op jit(solution)/shard_map/scatter-add | solution.py:37
  294.5 2.3 fusion.48
  297.5 1.3 collective-permute-start.16
  298.8 5.8 %collective-permute-start.17 = (f32[1,128,128]{2,1,0:T(8,128)S(1)}, f32[1,128,128]{2,1,0:T(8,128)S(1)}, u32[]{:S(2)}, u32[]{:S(2)}) collective-permute-start(f32[1,128,128]{2,1,0:T(8,128)S(1)} %get-tuple-element.68), channel_id=1, source_target_pairs={{0,1},{1,2},{2,3},{3,4},{4,5},{5,6},{6,7},{8,9},{9,10},{10,11},{11... | collective-permute-start | bytes 196616 | tf_op jit(solution)/shard_map/ppermute | solution.py:16
  304.8 1.6 collective-permute-done.17
  306.6 1.6 fusion.28
  308.2 5.3 %scatter_fusion.3 = f32[262144]{0:T(1024)} fusion(f32[262144]{0:T(1024)} %bitcast.155, s32[512]{0:T(512)S(1)} %bitcast.164, f32[512]{0:T(512)S(1)} %get-tuple-element.88), kind=kCustom, calls=%fused_computation.7 | custom fusion | flops 512 | bytes 8192 | tf_op jit(solution)/shard_map/scatter-add | solution.py:37
  313.5 4.4 %multiply_add_fusion = f32[16,128,128]{2,1,0:T(8,128)} fusion(f32[16,128,128]{2,1,0:T(8,128)} %bitcast.156, f32[16,128,128]{2,1,0:T(8,128)} %get-tuple-element.58, f32[16,128,128]{2,1,0:T(8,128)S(1)} %bitcast.144, f32[16,128,128]{2,1,0:T(8,128)} %get-tuple-element.56, f32[16,128,128]{2,1,0:T(8,128)S(1)} %bitcast.140, f32[16,128,128]{2,1,0:T(8,128)} %get-tuple-element.54, ...), kind=kLoop, calls=%fused_computation.125 | loop fusion | flops 1835008 | bytes 9437184 | tf_op jit(solution)/shard_map/add | solution.py:113
  317.8 2.4 broadcast_in_dim.15
  320.3 13.9 %dynamic_update_slice.3 = f32[16,256,256]{2,1,0:T(8,128)} dynamic-update-slice(f32[16,256,256]{2,1,0:T(8,128)} %broadcast_in_dim.15, f32[16,128,128]{2,1,0:T(8,128)S(1)} %copy-done.36, s32[]{:T(128)} %constant.95.clone.1, s32[]{:T(128)S(6)} %select_n.55, s32[]{:T(128)S(6)} %select_n.56) | dynamic-update-slice | bytes 2097156 | tf_op jit(solution)/shard_map/dynamic_update_slice | solution.py:116
  334.2 1.2 copy-done.17
  335.7 3.7 maximum_bitcast_fusion
  339.4 81.1 %reduce-scatter.2.cloned.1.call-done = f32[16,16,256]{2,1,0:T(8,128)} async-done(((f32[16,256,256]{2,1,0:T(8,128)}), f32[16,16,256]{2,1,0:T(8,128)}) %reduce-scatter.2.cloned.1.call-update) | async-done | bytes 262160 | tf_op jit(solution)/shard_map/reduce_scatter | solution.py:121
  (146 shorter events, 16.7 us)
Async XLA Ops:
  7.2 19.5 %copy-start = (s32[16,2]{0,1:T(2,128)S(1)}, s32[16,2]{0,1:T(2,128)}, u32[]{:S(2)}) copy-start(s32[16,2]{0,1:T(2,128)} %param.19) | copy-start | bytes 388
  12.6 8.2 %copy-start.32 = (f32[1,2,16,128,128]{4,3,2,1,0:T(8,128)S(1)}, f32[1,2,16,128,128]{4,3,2,1,0:T(8,128)}, u32[]{:S(2)}) copy-start(f32[1,2,16,128,128]{4,3,2,1,0:T(8,128)} %param.20) | copy-start | bytes 6291460
  12.6 17.3 %copy-start.45 = (s32[1,3]{1,0:T(1,128)S(1)}, s32[1,3]{1,0:T(1,128)}, u32[]{:S(2)}) copy-start(s32[1,3]{1,0:T(1,128)} %param.23) | copy-start | bytes 40
  12.6 20.4 %copy-start.38 = (f32[1,4]{1,0:T(1,128)S(1)}, f32[1,4]{1,0:T(1,128)}, u32[]{:S(2)}) copy-start(f32[1,4]{1,0:T(1,128)} %param.22) | copy-start | bytes 52
  12.6 23.7 %copy-start.44 = (s32[1,512,3]{1,0,2:T(1,128)S(1)}, s32[1,512,3]{1,0,2:T(1,128)}, u32[]{:S(2)}) copy-start(s32[1,512,3]{1,0,2:T(1,128)} %param.24) | copy-start | bytes 18436
  12.6 25.6 %copy-start.37 = (f32[1,4,512]{2,1,0:T(4,128)S(1)}, f32[1,4,512]{2,1,0:T(4,128)}, u32[]{:S(2)}) copy-start(f32[1,4,512]{2,1,0:T(4,128)} %param.25) | copy-start | bytes 24580
  12.6 118.6 %all-to-all-start = ((f32[16,2,16,16,256]{4,3,2,1,0:T(8,128)}), f32[16,2,16,16,256]{4,3,2,1,0:T(8,128)}, u32[]{:S(2)}, u32[]{:S(2)}) async-start(f32[16,2,16,16,256]{4,3,2,1,0:T(8,128)} %stack.15), calls=%async_computation | async-start | bytes 16777216 | tf_op jit(solution)/shard_map/all_to_all | solution.py:62
  20.8 399.7 %reduce-scatter.2.cloned.1.call-start = ((), (), s32[]{:S(2)}) async-start(), calls=%async_computation.2 | async-start | bytes 4456448 | tf_op jit(solution)/shard_map/reduce_scatter | solution.py:121
  20.8 124.3 %collective-permute-start.4 = (f32[1,128,128]{2,1,0:T(8,128)S(1)}, f32[1,128,128]{2,1,0:T(8,128)S(1)}, u32[]{:S(2)}, u32[]{:S(2)}) collective-permute-start(f32[1,128,128]{2,1,0:T(8,128)S(1)} %get-tuple-element.67), channel_id=1, source_target_pairs={{1,0},{2,1},{3,2},{4,3},{5,4},{6,5},{7,6},{9,8},{10,9},{11,10},{12... | collective-permute-start | bytes 196616 | tf_op jit(solution)/shard_map/ppermute | solution.py:17
  22.1 123.0 %collective-permute-start.5 = (f32[1,128,128]{2,1,0:T(8,128)S(1)}, f32[1,128,128]{2,1,0:T(8,128)S(1)}, u32[]{:S(2)}, u32[]{:S(2)}) collective-permute-start(f32[1,128,128]{2,1,0:T(8,128)S(1)} %get-tuple-element.66), channel_id=1, source_target_pairs={{0,1},{1,2},{2,3},{3,4},{4,5},{5,6},{6,7},{8,9},{9,10},{10,11},{11... | collective-permute-start | bytes 196616 | tf_op jit(solution)/shard_map/ppermute | solution.py:16
  135.6 10.4 %copy-start.24 = (f32[16,2,16,16,256]{4,3,0,2,1:T(8,128)}, f32[16,2,16,16,256]{4,3,0,2,1:T(8,128)S(1)}, u32[]{:S(2)}) copy-start(f32[16,2,16,16,256]{4,3,0,2,1:T(8,128)S(1)} %copy.12) | copy-start | bytes 25165828
  135.6 8.0 %copy-start.27 = (f32[16,128,128]{2,1,0:T(8,128)S(1)}, f32[16,128,128]{2,1,0:T(8,128)}, u32[]{:S(2)}) copy-start(f32[16,128,128]{2,1,0:T(8,128)} %slice_bitcast_fusion) | copy-start | bytes 3145732
  136.1 9.1 %collective-permute-start = (f32[1,128,128]{2,1,0:T(8,128)S(1)}, f32[1,128,128]{2,1,0:T(8,128)S(1)}, u32[]{:S(2)}, u32[]{:S(2)}) collective-permute-start(f32[1,128,128]{2,1,0:T(8,128)S(1)} %get-tuple-element.64), channel_id=1, source_target_pairs={{1,0},{2,1},{3,2},{4,3},{5,4},{6,5},{7,6},{9,8},{10,9},{11,10},{12... | collective-permute-start | bytes 196616 | tf_op jit(solution)/shard_map/ppermute | solution.py:17
  137.5 8.2 %collective-permute-start.1 = (f32[1,128,128]{2,1,0:T(8,128)S(1)}, f32[1,128,128]{2,1,0:T(8,128)S(1)}, u32[]{:S(2)}, u32[]{:S(2)}) collective-permute-start(f32[1,128,128]{2,1,0:T(8,128)S(1)} %get-tuple-element.65), channel_id=1, source_target_pairs={{0,1},{1,2},{2,3},{3,4},{4,5},{5,6},{6,7},{8,9},{9,10},{10,11},{11... | collective-permute-start | bytes 196616 | tf_op jit(solution)/shard_map/ppermute | solution.py:16
  145.1 13.6 %copy-start.2 = (f32[16,129,128]{2,1,0:T(8,128)}, f32[16,129,128]{2,1,0:T(8,128)S(1)}, u32[]{:S(2)}) copy-start(f32[16,129,128]{2,1,0:T(8,128)S(1)} %get-tuple-element.60) | copy-start | bytes 3170308
  145.1 2.0 copy-start.33
  149.9 8.7 %copy-start.9 = (f32[262144]{0:T(1024)}, f32[262144]{0:T(1024)S(1)}, u32[]{:S(2)}) copy-start(f32[262144]{0:T(1024)S(1)} %fusion.52) | copy-start | bytes 3145732
  149.9 17.8 %collective-permute-start.6 = (f32[1,128,128]{2,1,0:T(8,128)S(1)}, f32[1,128,128]{2,1,0:T(8,128)S(1)}, u32[]{:S(2)}, u32[]{:S(2)}) collective-permute-start(f32[1,128,128]{2,1,0:T(8,128)S(1)} %get-tuple-element.79), channel_id=1, source_target_pairs={{1,0},{2,1},{3,2},{4,3},{5,4},{6,5},{7,6},{9,8},{10,9},{11,10},{12... | collective-permute-start | bytes 196616 | tf_op jit(solution)/shard_map/ppermute | solution.py:17
  151.2 16.5 %collective-permute-start.7 = (f32[1,128,128]{2,1,0:T(8,128)S(1)}, f32[1,128,128]{2,1,0:T(8,128)S(1)}, u32[]{:S(2)}, u32[]{:S(2)}) collective-permute-start(f32[1,128,128]{2,1,0:T(8,128)S(1)} %get-tuple-element.78), channel_id=1, source_target_pairs={{0,1},{1,2},{2,3},{3,4},{4,5},{5,6},{6,7},{8,9},{9,10},{10,11},{11... | collective-permute-start | bytes 196616 | tf_op jit(solution)/shard_map/ppermute | solution.py:16
  167.7 2.1 copy-start.10
  167.7 2.2 copy-start.31
  175.6 8.6 %copy-start.12 = (f32[262144]{0:T(1024)}, f32[262144]{0:T(1024)S(1)}, u32[]{:S(2)}) copy-start(f32[262144]{0:T(1024)S(1)} %fusion.53) | copy-start | bytes 3145732
  175.6 17.6 %collective-permute-start.8 = (f32[1,128,128]{2,1,0:T(8,128)S(1)}, f32[1,128,128]{2,1,0:T(8,128)S(1)}, u32[]{:S(2)}, u32[]{:S(2)}) collective-permute-start(f32[1,128,128]{2,1,0:T(8,128)S(1)} %get-tuple-element.77), channel_id=1, source_target_pairs={{1,0},{2,1},{3,2},{4,3},{5,4},{6,5},{7,6},{9,8},{10,9},{11,10},{12... | collective-permute-start | bytes 196616 | tf_op jit(solution)/shard_map/ppermute | solution.py:17
  176.9 16.3 %collective-permute-start.9 = (f32[1,128,128]{2,1,0:T(8,128)S(1)}, f32[1,128,128]{2,1,0:T(8,128)S(1)}, u32[]{:S(2)}, u32[]{:S(2)}) collective-permute-start(f32[1,128,128]{2,1,0:T(8,128)S(1)} %get-tuple-element.76), channel_id=1, source_target_pairs={{0,1},{1,2},{2,3},{3,4},{4,5},{5,6},{6,7},{8,9},{9,10},{10,11},{11... | collective-permute-start | bytes 196616 | tf_op jit(solution)/shard_map/ppermute | solution.py:16
  182.2 2.0 copy-start.3
  193.2 2.1 copy-start.11
  193.2 2.2 copy-start.13
  193.2 2.5 copy-start.30
  201.1 8.7 %copy-start.15 = (f32[262144]{0:T(1024)}, f32[262144]{0:T(1024)S(1)}, u32[]{:S(2)}) copy-start(f32[262144]{0:T(1024)S(1)} %fusion.54) | copy-start | bytes 3145732
  201.1 17.8 %collective-permute-start.10 = (f32[1,128,128]{2,1,0:T(8,128)S(1)}, f32[1,128,128]{2,1,0:T(8,128)S(1)}, u32[]{:S(2)}, u32[]{:S(2)}) collective-permute-start(f32[1,128,128]{2,1,0:T(8,128)S(1)} %get-tuple-element.75), channel_id=1, source_target_pairs={{1,0},{2,1},{3,2},{4,3},{5,4},{6,5},{7,6},{9,8},{10,9},{11,10},{12... | collective-permute-start | bytes 196616 | tf_op jit(solution)/shard_map/ppermute | solution.py:17
  202.4 16.5 %collective-permute-start.11 = (f32[1,128,128]{2,1,0:T(8,128)S(1)}, f32[1,128,128]{2,1,0:T(8,128)S(1)}, u32[]{:S(2)}, u32[]{:S(2)}) collective-permute-start(f32[1,128,128]{2,1,0:T(8,128)S(1)} %get-tuple-element.74), channel_id=1, source_target_pairs={{0,1},{1,2},{2,3},{3,4},{4,5},{5,6},{6,7},{8,9},{9,10},{10,11},{11... | collective-permute-start | bytes 196616 | tf_op jit(solution)/shard_map/ppermute | solution.py:16
  207.8 2.0 copy-start.4
  218.9 2.1 copy-start.14
  218.9 2.2 copy-start.16
  218.9 2.5 copy-start.29
  221.4 5.1 %copy-start.5 = (f32[16,129,128]{2,1,0:T(8,128)S(1)}, f32[16,129,128]{2,1,0:T(8,128)}, u32[]{:S(2)}) copy-start(f32[16,129,128]{2,1,0:T(8,128)} %copy-done.2) | copy-start | bytes 3170308
  229.8 15.4 %copy-start.39 = (f32[1,1,512]{2,1,0:T(1,128)S(1)}, f32[1,1,512]{2,1,0:T(1,128)}, u32[]{:S(2)}) copy-start(f32[1,1,512]{2,1,0:T(1,128)} %get-tuple-element.84) | copy-start | bytes 6148
  229.8 15.4 %copy-start.40 = (f32[1,1,512]{2,1,0:T(1,128)S(1)}, f32[1,1,512]{2,1,0:T(1,128)}, u32[]{:S(2)}) copy-start(f32[1,1,512]{2,1,0:T(1,128)} %get-tuple-element.85) | copy-start | bytes 6148
  229.8 15.4 %copy-start.41 = (f32[512]{0:T(512)S(1)}, f32[512]{0:T(512)}, u32[]{:S(2)}) copy-start(f32[512]{0:T(512)} %gather_fusion.3) | copy-start | bytes 6148
  229.8 15.4 %copy-start.42 = (f32[512]{0:T(512)S(1)}, f32[512]{0:T(512)}, u32[]{:S(2)}) copy-start(f32[512]{0:T(512)} %gather_fusion.2) | copy-start | bytes 6148
  229.8 15.4 %copy-start.43 = (f32[512]{0:T(512)S(1)}, f32[512]{0:T(512)}, u32[]{:S(2)}) copy-start(f32[512]{0:T(512)} %gather_fusion.1) | copy-start | bytes 6148
  229.8 15.4 %copy-start.46 = (pred[512]{0:T(512)(128)(4,1)S(1)}, pred[512]{0:T(512)(128)(4,1)}, u32[]{:S(2)}) copy-start(pred[512]{0:T(512)(128)(4,1)} %and_reduce_fusion) | copy-start | bytes 1540
  238.7 6.7 %collective-permute-start.2 = (f32[1,128,128]{2,1,0:T(8,128)S(1)}, f32[1,128,128]{2,1,0:T(8,128)S(1)}, u32[]{:S(2)}, u32[]{:S(2)}) collective-permute-start(f32[1,128,128]{2,1,0:T(8,128)S(1)} %get-tuple-element.81), channel_id=1, source_target_pairs={{1,0},{2,1},{3,2},{4,3},{5,4},{6,5},{7,6},{9,8},{10,9},{11,10},{12... | collective-permute-start | bytes 196616 | tf_op jit(solution)/shard_map/ppermute | solution.py:17
  240.0 7.0 %collective-permute-start.3 = (f32[1,128,128]{2,1,0:T(8,128)S(1)}, f32[1,128,128]{2,1,0:T(8,128)S(1)}, u32[]{:S(2)}, u32[]{:S(2)}) collective-permute-start(f32[1,128,128]{2,1,0:T(8,128)S(1)} %get-tuple-element.80), channel_id=1, source_target_pairs={{0,1},{1,2},{2,3},{3,4},{4,5},{5,6},{6,7},{8,9},{9,10},{10,11},{11... | collective-permute-start | bytes 196616 | tf_op jit(solution)/shard_map/ppermute | solution.py:16
  245.3 3.7 copy-start.28
  245.3 3.7 copy-start.34
  259.4 7.4 %copy-start.6 = (f32[16,129,128]{2,1,0:T(8,128)S(1)}, f32[16,129,128]{2,1,0:T(8,128)}, u32[]{:S(2)}) copy-start(f32[16,129,128]{2,1,0:T(8,128)} %copy-done.2) | copy-start | bytes 3170308
  260.1 7.1 %collective-permute-start.12 = (f32[1,128,128]{2,1,0:T(8,128)S(1)}, f32[1,128,128]{2,1,0:T(8,128)S(1)}, u32[]{:S(2)}, u32[]{:S(2)}) collective-permute-start(f32[1,128,128]{2,1,0:T(8,128)S(1)} %get-tuple-element.73), channel_id=1, source_target_pairs={{1,0},{2,1},{3,2},{4,3},{5,4},{6,5},{7,6},{9,8},{10,9},{11,10},{12... | collective-permute-start | bytes 196616 | tf_op jit(solution)/shard_map/ppermute | solution.py:17
  261.4 7.3 %collective-permute-start.13 = (f32[1,128,128]{2,1,0:T(8,128)S(1)}, f32[1,128,128]{2,1,0:T(8,128)S(1)}, u32[]{:S(2)}, u32[]{:S(2)}) collective-permute-start(f32[1,128,128]{2,1,0:T(8,128)S(1)} %get-tuple-element.72), channel_id=1, source_target_pairs={{0,1},{1,2},{2,3},{3,4},{4,5},{5,6},{6,7},{8,9},{9,10},{10,11},{11... | collective-permute-start | bytes 196616 | tf_op jit(solution)/shard_map/ppermute | solution.py:16
  267.0 1.9 copy-start.18
  267.0 1.9 copy-start.35
  277.9 8.0 %copy-start.7 = (f32[16,129,128]{2,1,0:T(8,128)S(1)}, f32[16,129,128]{2,1,0:T(8,128)}, u32[]{:S(2)}) copy-start(f32[16,129,128]{2,1,0:T(8,128)} %copy-done.2) | copy-start | bytes 3170308
  278.6 7.5 %collective-permute-start.14 = (f32[1,128,128]{2,1,0:T(8,128)S(1)}, f32[1,128,128]{2,1,0:T(8,128)S(1)}, u32[]{:S(2)}, u32[]{:S(2)}) collective-permute-start(f32[1,128,128]{2,1,0:T(8,128)S(1)} %get-tuple-element.71), channel_id=1, source_target_pairs={{1,0},{2,1},{3,2},{4,3},{5,4},{6,5},{7,6},{9,8},{10,9},{11,10},{12... | collective-permute-start | bytes 196616 | tf_op jit(solution)/shard_map/ppermute | solution.py:17
  279.9 7.7 %collective-permute-start.15 = (f32[1,128,128]{2,1,0:T(8,128)S(1)}, f32[1,128,128]{2,1,0:T(8,128)S(1)}, u32[]{:S(2)}, u32[]{:S(2)}) collective-permute-start(f32[1,128,128]{2,1,0:T(8,128)S(1)} %get-tuple-element.70), channel_id=1, source_target_pairs={{0,1},{1,2},{2,3},{3,4},{4,5},{5,6},{6,7},{8,9},{9,10},{10,11},{11... | collective-permute-start | bytes 196616 | tf_op jit(solution)/shard_map/ppermute | solution.py:16
  286.1 1.7 copy-start.19
  286.1 1.7 copy-start.21
  296.8 7.8 %copy-start.8 = (f32[16,129,128]{2,1,0:T(8,128)S(1)}, f32[16,129,128]{2,1,0:T(8,128)}, u32[]{:S(2)}) copy-start(f32[16,129,128]{2,1,0:T(8,128)} %copy-done.2) | copy-start | bytes 3170308
  297.5 7.4 %collective-permute-start.16 = (f32[1,128,128]{2,1,0:T(8,128)S(1)}, f32[1,128,128]{2,1,0:T(8,128)S(1)}, u32[]{:S(2)}, u32[]{:S(2)}) collective-permute-start(f32[1,128,128]{2,1,0:T(8,128)S(1)} %get-tuple-element.69), channel_id=1, source_target_pairs={{1,0},{2,1},{3,2},{4,3},{5,4},{6,5},{7,6},{9,8},{10,9},{11,10},{12... | collective-permute-start | bytes 196616 | tf_op jit(solution)/shard_map/ppermute | solution.py:17
  298.8 7.7 %collective-permute-start.17 = (f32[1,128,128]{2,1,0:T(8,128)S(1)}, f32[1,128,128]{2,1,0:T(8,128)S(1)}, u32[]{:S(2)}, u32[]{:S(2)}) collective-permute-start(f32[1,128,128]{2,1,0:T(8,128)S(1)} %get-tuple-element.68), channel_id=1, source_target_pairs={{0,1},{1,2},{2,3},{3,4},{4,5},{5,6},{6,7},{8,9},{9,10},{10,11},{11... | collective-permute-start | bytes 196616 | tf_op jit(solution)/shard_map/ppermute | solution.py:16
  304.7 1.9 copy-start.22
  304.7 1.9 copy-start.23
  308.2 5.3 %copy-start.20 = (f32[262144]{0:T(1024)S(1)}, f32[262144]{0:T(1024)}, u32[]{:S(2)}) copy-start(f32[262144]{0:T(1024)} %scatter_fusion) | copy-start | bytes 3145732
  317.8 2.4 copy-start.36
  335.7 84.8 %copy-start.1 = (s32[16,2]{0,1:T(2,128)S(1)}, s32[16,2]{0,1:T(2,128)}, u32[]{:S(2)}) copy-start(s32[16,2]{0,1:T(2,128)} %param.19) | copy-start | bytes 388
  (3 other events, 4.1 us)
Sparse Core Ops, SparseCore 0:
  334.3 86.1 reduce-scatter.1
